TPU v7x, 256 devices: a whole 4x4x8 slice. The times are simulated.
256 devices in a mesh: lon: 32 (over x_hi, z, core), tp: 8 (over y, x_lo).
Axes of the slice: x: 4 (x_hi: 2, x_lo: 2; x = x_hi * 2 + x_lo), y: 4, z: 8, core: 2. Of those that a mesh axis runs over, the one named last changes fastest.
Arguments:
- queries: bfloat16 [16384, 3072], P('lon', 'tp'), may hold values from -81 to 81
- keys: bfloat16 [16384, 3072], P('lon', 'tp'), may hold values from -9 to 9
- values: bfloat16 [16384, 3072], P('lon', 'tp'), may hold values from -6 to 6
- out_grad: bfloat16 [16384, 3072], P('lon', 'tp'), may hold values from -6 to 6
- out_weight: bfloat16 [3072, 3072], P('tp'), may hold values from -0.109375 to 0.109375
- window: int32 [128, 9], replicated, may hold values from 0 to 127, as said below
- counts: int32 [128], replicated, may hold values from 1 to 9
Outputs:
- query_grad: bfloat16 [16384, 3072], P('lon', 'tp')
- key_grad: bfloat16 [16384, 3072], P('lon', 'tp')
- value_grad: bfloat16 [16384, 3072], P('lon', 'tp')
- weight_grad: bfloat16 [3072, 3072], P('tp', 'lon')
Inputs may be any that keep to these rules, and one draw needn't show every extreme that they name: `window`: for tile g (stripe g // 4, latitude row g % 4) the first counts[g] entries are distinct tiles whose stripe differs from g's by at most one around the loop of 32 stripes and whose latitude row differs by at most one; the first entry is g itself; later entries repeat g.
All inputs are finite; a program needn't handle non-finite values.
Results may differ from a plain program's by a relative error of at most 0.034.
Values may be sent and summed in bfloat16 or wider, within the bound.
A program may use at most 128 MiB of HBM per device.

v0:
```python
import jax
import jax.numpy as jnp
from jax import lax
from jax.sharding import PartitionSpec as P

HEAD_DIM = 128
TILE = 128


neg_fill = -1e30


def extended(shard, sides, width):
    for axis, dim in sides:
        devices, length = (lax.axis_size(axis), shard.shape[dim])
        up = [(i, (i + 1) % devices) for i in range(devices)]
        down = [(j, i) for i, j in up]
        last = lax.slice_in_dim(shard, length - width, length, axis=dim)
        leading = lax.slice_in_dim(shard, 0, width, axis=dim)
        before = lax.ppermute(last, axis, up)
        after = lax.ppermute(leading, axis, down)
        shard = jnp.concatenate([before, shard, after], axis=dim)
    return shard


def passed_along(block, axis, distance):
    devices = range(lax.axis_size(axis))
    route = [((i - distance) % len(devices), i) for i in devices]
    return lax.ppermute(block, axis, route)


def tile_lists(window, counts, first_tile, tile_count):
    tile_rows = lax.dynamic_slice_in_dim(window, first_tile, tile_count, 0)
    lengths = lax.dynamic_slice_in_dim(counts, first_tile, tile_count, 0)
    slots = jnp.arange(window.shape[1], dtype=jnp.int32)
    return (tile_rows, slots[None, :] < lengths[:, None])


def allowed_tiles(tile_rows, slot_live, target_ids):
    hits = (tile_rows[:, :, None] == target_ids[None, None, :]) & slot_live[:, :, None]
    return jnp.any(hits, axis=1)


def spread_tiles(tile_mask):
    return jnp.repeat(jnp.repeat(tile_mask, TILE, axis=0), TILE, axis=1)


def body(queries, keys, values, out_grad, out_weight, window, counts):
    tokens, col_width = queries.shape
    head_count = col_width // HEAD_DIM
    tile_count = tokens // TILE
    stripe_count = lax.axis_size("lon")
    stripe_index = lax.axis_index("lon")
    inv_root = HEAD_DIM ** (-0.5)
    offsets = jnp.array([-1, 0, 1], dtype=jnp.int32)
    near_stripes = (stripe_index + offsets) % stripe_count
    lat_rows = jnp.arange(tile_count, dtype=jnp.int32)
    near_ids = (near_stripes[:, None] * tile_count + lat_rows[None, :]).reshape(-1)
    own_rows, own_live = tile_lists(window, counts, stripe_index * tile_count, tile_count)
    key_mask = spread_tiles(allowed_tiles(own_rows, own_live, near_ids))
    paired = jnp.concatenate([keys, values], axis=1)
    neighbours = extended(paired, (("lon", 0),), tokens)
    near_keys = neighbours[:, :col_width]
    near_values = neighbours[:, col_width:]
    saved = []
    outputs = []
    for head_no in range(head_count):
        columns = slice(head_no * HEAD_DIM, (head_no + 1) * HEAD_DIM)
        scores = (
            jnp.einsum(
                "qd,kd->qk",
                queries[:, columns],
                near_keys[:, columns],
                preferred_element_type=jnp.float32,
            )
            * inv_root
        )
        scores = jnp.where(key_mask, scores, neg_fill)
        row_max = jnp.max(scores, axis=1, keepdims=True)
        weights = jnp.exp(scores - row_max)
        row_total = jnp.sum(weights, axis=1, keepdims=True)
        probs = weights / row_total
        probs_low = probs.astype(jnp.bfloat16)
        saved.append((probs, probs_low, row_max, row_total))
        outputs.append(
            jnp.dot(probs_low, near_values[:, columns], preferred_element_type=jnp.float32).astype(
                jnp.bfloat16
            )
        )
    attended = jnp.concatenate(outputs, axis=1)
    piece = lax.all_gather(out_grad, "tp", axis=1, tiled=True)
    grad_total = jnp.einsum("tc,hc->th", piece, out_weight, preferred_element_type=jnp.float32)
    column_part = jnp.einsum("th,tc->hc", attended, piece, preferred_element_type=jnp.float32)
    grad_total, column_store = (grad_total, column_part)
    weight_grad = lax.psum_scatter(column_store, "lon", scatter_dimension=1, tiled=True).astype(
        jnp.bfloat16
    )
    grad_attended = grad_total.astype(jnp.bfloat16)
    query_parts = []
    key_parts = []
    value_parts = []
    for head_no in range(head_count):
        columns = slice(head_no * HEAD_DIM, (head_no + 1) * HEAD_DIM)
        probs, probs_low, row_max, row_total = saved[head_no]
        grad_here = grad_attended[:, columns]
        delta = jnp.sum(
            grad_here.astype(jnp.float32) * attended[:, columns].astype(jnp.float32),
            axis=1,
            keepdims=True,
        )
        grad_probs = jnp.einsum(
            "qd,kd->qk", grad_here, near_values[:, columns], preferred_element_type=jnp.float32
        )
        grad_scores = (probs * (grad_probs - delta)).astype(jnp.bfloat16)
        query_parts.append(
            (
                jnp.dot(grad_scores, near_keys[:, columns], preferred_element_type=jnp.float32)
                * inv_root
            ).astype(jnp.bfloat16)
        )
        key_parts.append(
            jnp.einsum(
                "qk,qd->kd", grad_scores, queries[:, columns], preferred_element_type=jnp.float32
            )
            * inv_root
        )
        value_parts.append(
            jnp.einsum("qk,qd->kd", probs_low, grad_here, preferred_element_type=jnp.float32)
        )
    query_grad = jnp.concatenate(query_parts, axis=1)
    near_terms = jnp.concatenate(key_parts + value_parts, axis=1)
    lower_terms = near_terms[:tokens]
    middle_terms = near_terms[tokens : 2 * tokens]
    upper_terms = near_terms[2 * tokens :]
    from_left = passed_along(upper_terms, "lon", 1)
    from_right = passed_along(lower_terms, "lon", -1)
    key_terms = middle_terms + from_left + from_right
    key_grad = key_terms[:, :col_width].astype(jnp.bfloat16)
    value_grad = key_terms[:, col_width:].astype(jnp.bfloat16)
    return (query_grad, key_grad, value_grad, weight_grad)


def solution(mesh):
    in_specs = (
        P("lon", "tp"),
        P("lon", "tp"),
        P("lon", "tp"),
        P("lon", "tp"),
        P("tp", None),
        P(),
        P(),
    )
    out_specs = (P("lon", "tp"), P("lon", "tp"), P("lon", "tp"), P("tp", "lon"))
    return jax.shard_map(body, mesh=mesh, in_specs=in_specs, out_specs=out_specs, check_vma=False)
```

profile of v0, /device:TPU:1, one launch (start us, length us, event | category | flops | bytes accessed | tf_op | source)
XLA Modules:
  0.0 234.7 jit_solution(3816046974765845468)
XLA Ops:
  7.2 0.0 copy-start
  7.2 0.0 all-gather.2.cloned.1.call-start
  7.2 0.7 all-gather.2.cloned.1.call-update
  7.9 0.0 reduce-scatter.2.cloned.1.call-start
  8.0 1.1 constant_dynamic-update-slice_fusion.1
  9.1 1.1 constant_dynamic-update-slice_fusion
  10.1 3.3 %collective-permute-start.1 = (bf16[512,768]{1,0:T(8,128)(2,1)S(1)}, bf16[512,768]{1,0:T(8,128)(2,1)}, u32[]{:S(2)}, u32[]{:S(2)}) collective-permute-start(bf16[512,768]{1,0:T(8,128)(2,1)S(1)} %constant_dynamic-update-slice_fusion), channel_id=1, source_target_pairs={{8,0},{16,8},{24,16},{32,24},{40,32},{48,40},{56,48},{64,56},{72,6... | collective-permute-start | bytes 2359304 | tf_op jit(solution)/shard_map/ppermute | solution.py:21
  13.4 0.7 fusion.57
  14.1 0.1 iota_add_fusion
  14.2 0.1 add.51
  14.3 0.7 dynamic_slice.7
  15.0 0.8 constant_dynamic-slice_fusion
  15.8 0.1 and_reduce_fusion
  15.9 0.1 copy.19
  16.0 0.1 broadcast_bitcast_fusion
  16.1 6.9 %collective-permute-done.1 = bf16[512,768]{1,0:T(8,128)(2,1)} collective-permute-done((bf16[512,768]{1,0:T(8,128)(2,1)S(1)}, bf16[512,768]{1,0:T(8,128)(2,1)}, u32[]{:S(2)}, u32[]{:S(2)}) %collective-permute-start.1) | collective-permute-done | bytes 786464 | tf_op jit(solution)/shard_map/ppermute | solution.py:21
  23.0 1.5 pad_maximum_fusion
  24.6 0.6 fusion.63
  25.1 0.6 fusion.62
  25.7 0.6 fusion.61
  26.3 0.5 fusion.14
  26.8 0.5 fusion.12
  27.3 0.5 fusion.10
  27.8 0.5 fusion.23
  28.4 0.4 convolution_convert_fusion.1
  28.8 0.5 fusion.24
  29.3 0.2 copy-done.7
  29.5 0.4 convolution_convert_fusion.2
  30.0 0.7 copy-done.9
  30.6 1.6 fusion.25
  32.3 61.6 %all-gather.2.cloned.1.call-done = bf16[512,3072]{1,0:T(8,128)(2,1)} async-done(((bf16[512,384]{1,0:T(8,128)(2,1)}), bf16[512,3072]{1,0:T(8,128)(2,1)}) %all-gather.2.cloned.1.call-update) | async-done | bytes 3145744 | tf_op jit(solution)/shard_map/all_gather | solution.py:91
  93.9 3.4 %convolution_convert_fusion = bf16[512,384]{0,1:T(8,128)(2,1)S(1)} fusion(bf16[512,3072]{1,0:T(8,128)(2,1)} %all-gather.2.cloned.1.call-done, bf16[384,3072]{1,0:T(8,128)(2,1)S(1)} %copy-done), kind=kOutput, calls=%fused_computation.40 | convolution fusion | flops 1208156160 | bytes 5898240 | tf_op jit(solution)/shard_map/tc,hc->th/dot_general | solution.py:92
  97.3 2.3 multiply_reduce_fusion.2
  99.6 4.0 %fusion.26 = f32[384,3072]{0,1:T(8,128)} fusion(bf16[512,3072]{1,0:T(8,128)(2,1)S(1)} %copy-done.15, bf16[512,128]{0,1:T(8,128)(2,1)S(1)} %convolution_convert_fusion.1, bf16[512,128]{0,1:T(8,128)(2,1)S(1)} %convolution_convert_fusion.2, bf16[512,128]{0,1:T(8,128)(2,1)S(1)} %get-tuple-element.25), kind=kOutput, calls=%fused_computation.54 | convolution fusion | flops 1209139200 | bytes 8257536 | tf_op jit(solution)/shard_map/th,tc->hc/dot_general | solution.py:93
  103.6 0.0 reduce-scatter.2.cloned.1.call-update
  103.6 0.6 copy-done.20
  104.2 0.0 copy-done.23
  104.3 2.9 %fusion.8 = bf16[512,1536]{0,1:T(8,128)(2,1)S(1)} fusion(f32[512]{0:T(512)S(1)} %copy-done.23, f32[512]{0:T(512)S(1)} %copy-done.20, f32[512,1536]{0,1:T(8,128)} %copy-done.5, f32[512]{0:T(512)S(1)} %get-tuple-element.19, bf16[1536,768]{1,0:T(8,128)(2,1)} %copy-done.13, bf16[512,384]{0,1:T(8,128)(2,1)S(1)} %convolution_convert_fusion), kind=kOutput, calls=%fused_computation.20 | convolution fusion | flops 205258752 | bytes 5249024 | tf_op jit(solution)/shard_map/qd,kd->qk/dot_general | solution.py:111
  107.2 0.7 fusion.17
  107.9 0.1 copy-done.14
  108.0 0.8 fusion.7
  108.8 0.7 fusion.16
  109.4 0.5 copy-done.2
  110.0 1.0 fusion.6
  111.0 0.7 fusion.15
  111.6 0.6 convolution_dynamic-update-slice_fusion.2
  112.3 0.2 copy-done.10
  112.5 0.6 convolution_dynamic-update-slice_fusion.1
  113.2 0.6 convolution_dynamic-update-slice_fusion
  113.8 2.2 fusion.59
  116.0 0.9 copy-done.6
  116.9 0.5 collective-permute-start.3
  117.4 0.4 fusion.20
  117.9 0.4 fusion.21
  118.3 0.4 fusion.22
  118.7 0.9 copy.23
  119.7 14.9 %collective-permute-done.2 = f32[512,768]{0,1:T(8,128)} collective-permute-done((f32[512,768]{0,1:T(8,128)}, f32[512,768]{0,1:T(8,128)}, u32[]{:S(2)}, u32[]{:S(2)}) %collective-permute-start.2) | collective-permute-done | bytes 1572896 | tf_op jit(solution)/shard_map/ppermute | solution.py:29
  134.6 2.8 %collective-permute-done.3 = f32[512,768]{0,1:T(8,128)} collective-permute-done((f32[512,768]{0,1:T(8,128)}, f32[512,768]{0,1:T(8,128)}, u32[]{:S(2)}, u32[]{:S(2)}) %collective-permute-start.3) | collective-permute-done | bytes 1572896 | tf_op jit(solution)/shard_map/ppermute | solution.py:29
  137.4 2.9 %fusion.19 = bf16[512,768]{0,1:T(8,128)(2,1)S(1)} fusion(f32[512,768]{0,1:T(8,128)} %collective-permute-done.3, f32[512,768]{0,1:T(8,128)} %collective-permute-done.2, f32[1536,768]{0,1:T(8,128)} %copy-done.6), kind=kLoop, calls=%fused_computation.39 | loop fusion | flops 1179648 | bytes 5505024 | tf_op jit(solution)/shard_map/convert.1
  140.3 0.1 fusion.60
  140.3 0.9 copy.25
  141.3 0.9 copy.24
  142.2 84.1 %reduce-scatter.2.cloned.1.call-done = f32[384,96]{0,1:T(8,128)} async-done(((f32[384,3072]{0,1:T(8,128)}), f32[384,96]{0,1:T(8,128)}) %reduce-scatter.2.cloned.1.call-update) | async-done | bytes 147472 | tf_op jit(solution)/shard_map/reduce_scatter | solution.py:95
  226.3 1.6 convert_element_type.81
  (46 shorter events, 0.1 us)
Async XLA Ops:
  7.2 86.7 %copy-start = (bf16[384,3072]{1,0:T(8,128)(2,1)S(1)}, bf16[384,3072]{1,0:T(8,128)(2,1)}, u32[]{:S(2)}) copy-start(bf16[384,3072]{1,0:T(8,128)(2,1)} %param.12) | copy-start | bytes 7077892
  7.2 86.7 %all-gather.2.cloned.1.call-start = ((), (), s32[]{:S(2)}) async-start(), calls=%async_computation.1 | async-start | bytes 3538944 | tf_op jit(solution)/shard_map/all_gather | solution.py:91
  7.9 16.6 %copy-start.16 = (bf16[512,384]{1,0:T(8,128)(2,1)S(1)}, bf16[512,384]{1,0:T(8,128)(2,1)}, u32[]{:S(2)}) copy-start(bf16[512,384]{1,0:T(8,128)(2,1)} %param.8) | copy-start | bytes 1179652
  7.9 218.4 %reduce-scatter.2.cloned.1.call-start = ((), (), s32[]{:S(2)}) async-start(), calls=%async_computation.2 | async-start | bytes 4866048 | tf_op jit(solution)/shard_map/reduce_scatter | solution.py:95
  10.1 12.9 %collective-permute-start.1 = (bf16[512,768]{1,0:T(8,128)(2,1)S(1)}, bf16[512,768]{1,0:T(8,128)(2,1)}, u32[]{:S(2)}, u32[]{:S(2)}) collective-permute-start(bf16[512,768]{1,0:T(8,128)(2,1)S(1)} %constant_dynamic-update-slice_fusion), channel_id=1, source_target_pairs={{8,0},{16,8},{24,16},{32,24},{40,32},{48,40},{56,48},{64,56},{72,6... | collective-permute-start | bytes 2359304 | tf_op jit(solution)/shard_map/ppermute | solution.py:21
  13.4 9.6 %collective-permute-start = (bf16[512,768]{1,0:T(8,128)(2,1)S(1)}, bf16[512,768]{1,0:T(8,128)(2,1)}, u32[]{:S(2)}, u32[]{:S(2)}) collective-permute-start(bf16[512,768]{1,0:T(8,128)(2,1)S(1)} %constant_dynamic-update-slice_fusion), channel_id=1, source_target_pairs={{0,8},{8,16},{16,24},{24,32},{32,40},{40,48},{48,56},{56,64},{64,7... | collective-permute-start | bytes 2359304 | tf_op jit(solution)/shard_map/ppermute | solution.py:20
  24.5 4.8 %copy-start.13 = (bf16[1536,768]{1,0:T(8,128)(2,1)}, bf16[1536,768]{1,0:T(8,128)(2,1)S(1)}, u32[]{:S(2)}) copy-start(bf16[1536,768]{1,0:T(8,128)(2,1)S(1)} %pad_maximum_fusion) | copy-start | bytes 7077892
  25.1 2.7 %copy-start.1 = (f32[512,1536]{0,1:T(8,128)}, f32[512,1536]{0,1:T(8,128)S(1)}, u32[]{:S(2)}) copy-start(f32[512,1536]{0,1:T(8,128)S(1)} %get-tuple-element.24) | copy-start | bytes 9437188
  25.7 3.0 %copy-start.3 = (f32[512,1536]{0,1:T(8,128)}, f32[512,1536]{0,1:T(8,128)S(1)}, u32[]{:S(2)}) copy-start(f32[512,1536]{0,1:T(8,128)S(1)} %get-tuple-element.22) | copy-start | bytes 9437188
  26.3 3.6 %copy-start.5 = (f32[512,1536]{0,1:T(8,128)}, f32[512,1536]{0,1:T(8,128)S(1)}, u32[]{:S(2)}) copy-start(f32[512,1536]{0,1:T(8,128)S(1)} %get-tuple-element.20) | copy-start | bytes 9437188
  27.3 1.5 copy-start.17
  27.8 2.1 copy-start.19
  28.3 1.2 copy-start.7
  29.5 1.1 copy-start.9
  93.9 3.4 %copy-start.11 = (bf16[512,1536]{0,1:T(8,128)(2,1)S(1)}, bf16[512,1536]{0,1:T(8,128)(2,1)}, u32[]{:S(2)}) copy-start(bf16[512,1536]{0,1:T(8,128)(2,1)} %fusion.25) | copy-start | bytes 4718596
  97.3 2.3 copy-start.15
  103.6 0.7 copy-start.20
  103.6 0.7 copy-start.23
  104.3 3.6 %copy-start.4 = (f32[512,1536]{0,1:T(8,128)S(1)}, f32[512,1536]{0,1:T(8,128)}, u32[]{:S(2)}) copy-start(f32[512,1536]{0,1:T(8,128)} %copy-done.3) | copy-start | bytes 9437188
  104.3 3.7 %copy-start.14 = (bf16[1536,768]{1,0:T(8,128)(2,1)S(1)}, bf16[1536,768]{1,0:T(8,128)(2,1)}, u32[]{:S(2)}) copy-start(bf16[1536,768]{1,0:T(8,128)(2,1)} %copy-done.13) | copy-start | bytes 7077892
  104.3 3.7 %copy-start.18 = (f32[512]{0:T(512)S(1)}, f32[512]{0:T(512)}, u32[]{:S(2)}) copy-start(f32[512]{0:T(512)} %copy-done.17) | copy-start | bytes 6148
  104.3 3.7 %copy-start.22 = (f32[512]{0:T(512)S(1)}, f32[512]{0:T(512)}, u32[]{:S(2)}) copy-start(f32[512]{0:T(512)} %get-tuple-element.13) | copy-start | bytes 6148
  108.0 2.0 copy-start.2
  108.0 2.0 copy-start.21
  110.0 1.7 copy-start.12
  110.9 1.6 copy-start.10
  110.9 2.2 copy-start.8
  113.8 3.1 %copy-start.6 = (f32[1536,768]{0,1:T(8,128)}, f32[1536,768]{0,1:T(8,128)S(1)}, u32[]{:S(2)}) copy-start(f32[1536,768]{0,1:T(8,128)S(1)} %convolution_dynamic-update-slice_fusion) | copy-start | bytes 14155780
  116.9 17.7 %collective-permute-start.2 = (f32[512,768]{0,1:T(8,128)}, f32[512,768]{0,1:T(8,128)}, u32[]{:S(2)}, u32[]{:S(2)}) collective-permute-start(f32[512,768]{0,1:T(8,128)} %get-tuple-element.15), channel_id=1, source_target_pairs={{248,0},{0,8},{8,16},{16,24},{24,32},{32,40},{40,48},{48,56},{56,6... | collective-permute-start | bytes 4718600 | tf_op jit(solution)/shard_map/ppermute | solution.py:29
  116.9 20.5 %collective-permute-start.3 = (f32[512,768]{0,1:T(8,128)}, f32[512,768]{0,1:T(8,128)}, u32[]{:S(2)}, u32[]{:S(2)}) collective-permute-start(f32[512,768]{0,1:T(8,128)} %get-tuple-element.16), channel_id=1, source_target_pairs={{8,0},{16,8},{24,16},{32,24},{40,32},{48,40},{56,48},{64,56},{72,6... | collective-permute-start | bytes 4718600 | tf_op jit(solution)/shard_map/ppermute | solution.py:29
Sparse Core Ops, SparseCore 0:
  9.8 83.9 all-gather.1
  103.7 122.5 reduce-scatter.1
where the time goes:
time: 238 us; the launch traced here: 235 us
  waiting for transfers between devices  171 us (72%)
  matrix products  22.1 us (9%)
  between operations  14.4 us (6%)
  local copies, waits for them, and re-layouts  12.3 us (5%)
  other arithmetic  11 us (5%)
  starting transfers between devices  3.91 us (2%)
    reduce_scatter x1, waiting for transfers between devices, body(): lax.psum_scatter(column_store, 'lon', scatter_dimension=1, tiled=True)  84.1 us
    all_gather x1, waiting for transfers between devices, body(): piece = lax.all_gather(out_grad, 'tp', axis=1, tiled=True)  61.6 us
    ppermute x2, waiting for transfers between devices, passed_along(): return lax.ppermute(block, axis, route)  17.7 us
    unnamed x55, local copies, waits for them, and re-layouts  7.28 us
    ppermute x1, waiting for transfers between devices, extended(): after = lax.ppermute(leading, axis, down)  6.9 us
  transfers between devices with their start and end apart: 6, of which 5 were waited for; matrix products, arithmetic and copies ran while one was open for 13% of the time, Pallas kernels for 0%

commit v1 on v0

v1 whole, which is shorter than its diff:
```python
import jax
import jax.numpy as jnp
from jax import lax
from jax.experimental import pallas as pl
from jax.experimental.pallas import tpu as pltpu
from jax.sharding import PartitionSpec as P

MESH = pl.DeviceIdType.MESH
F32 = jnp.float32
BF16 = jnp.bfloat16
HEAD_DIM = 128
TILE = 128
HEADS_HERE = 3
TOK = 512
COLS = HEADS_HERE * HEAD_DIM
SPAN = 3 * TILE
HALF = 2 * TILE
WIN = 9
LON = 32
TP = 8
STRIP = 96
INV_ROOT = HEAD_DIM ** -0.5
LOG2E = 1.4426950408889634
NEG = -1e30

NT = (((1,), (1,)), ((), ()))


def dot(a, b):
    return jnp.dot(a, b, preferred_element_type=F32)


def kernel(
    win_ref, cnt_ref, q_hbm, k_hbm, v_hbm, og_hbm, w_hbm,
    dq_ref, dk_ref, dv_ref, wg_ref,
    q_v, k_all, v_all, og_v, w_v, og_t, k_t, v_t, prob, scores, bias,
    att_t, att, inv_sum, delta, do_acc, do_t, do_n, dq_acc, pair_acc,
    own_pair, pair_out, pair_in, wg_full, wg_own, core_out, core_in,
    up_out, up_in, down_out, down_in, x_out, x_in,
    loc_sem, halo_s, halo_r, ag_s, ag_r, pair_s, pair_r, core_s, core_r,
    up_s, up_r, down_s, down_r, x_s, x_r,
):
    lon = lax.axis_index("lon")
    tp = lax.axis_index("tp")
    x_hi = lax.div(lon, 16)
    z = lax.rem(lax.div(lon, 2), 8)
    core = lax.rem(lon, 2)
    y = lax.div(tp, 2)
    x_lo = lax.rem(tp, 2)

    right = {"lon": lax.rem(lon + 1, LON)}
    left = {"lon": lax.rem(lon + LON - 1, LON)}
    twin = {"lon": lon + 1 - 2 * core}
    z_up = {"lon": x_hi * 16 + lax.rem(z + 1, 8) * 2 + core}
    z_down = {"lon": x_hi * 16 + lax.rem(z + 7, 8) * 2 + core}
    x_far = {"lon": lax.rem(lon + 16, LON)}
    y_p = lax.rem(y + 1, 4)
    y_m = lax.rem(y + 3, 4)
    y_2 = lax.rem(y + 2, 4)
    s_x = y * 2 + 1 - x_lo
    s_p = y_p * 2 + x_lo
    s_m = y_m * 2 + x_lo
    s_2 = y_2 * 2 + x_lo
    s_px = y_p * 2 + 1 - x_lo
    s_mx = y_m * 2 + 1 - x_lo
    s_2x = y_2 * 2 + 1 - x_lo
    to_x, to_p, to_m = {"tp": s_x}, {"tp": s_p}, {"tp": s_m}

    barrier = pltpu.get_barrier_semaphore()
    for other in (right, left, z_up, z_down, x_far, to_x, to_p, to_m):
        pl.semaphore_signal(barrier, inc=1, device_id=other, device_id_type=MESH)

    local = [
        pltpu.make_async_copy(src, dst, loc_sem.at[i])
        for i, (src, dst) in enumerate(
            ((og_hbm, og_v), (q_hbm, q_v), (k_hbm, k_all.at[1]), (v_hbm, v_all.at[1]), (w_hbm, w_v))
        )
    ]
    for copy in local:
        copy.start()
    local[0].wait()
    og_t[tp] = og_v[...].T

    def remote(src, dst, send, recv, to):
        return pltpu.make_async_remote_copy(
            src_ref=src, dst_ref=dst, send_sem=send, recv_sem=recv, device_id=to, device_id_type=MESH
        )

    def gather(number, slot, half, to):
        block = og_t.at[slot, pl.ds(half * 192, 192)]
        return remote(block, block, ag_s.at[number], ag_r.at[number], to)

    pl.semaphore_wait(barrier, 8)
    x0 = [gather(h, tp, h, to_x) for h in range(2)]
    p0 = [gather(2 + h, tp, h, to_p) for h in range(2)]
    m0 = [gather(4 + h, tp, h, to_m) for h in range(2)]
    x1 = [gather(6 + h, s_p, h, to_x) for h in range(2)]
    m1 = gather(8, s_p, 0, to_m)
    p1 = gather(9, s_m, 1, to_p)
    p2 = [gather(10 + h, s_x, h, to_p) for h in range(2)]
    m2 = [gather(12 + h, s_px, h, to_m) for h in range(2)]
    halo = [
        remote(k_hbm, k_all.at[0], halo_s.at[0], halo_r.at[0], right),
        remote(k_hbm, k_all.at[2], halo_s.at[1], halo_r.at[1], left),
        remote(v_hbm, v_all.at[0], halo_s.at[2], halo_r.at[2], right),
        remote(v_hbm, v_all.at[2], halo_s.at[3], halo_r.at[3], left),
    ]
    for h in range(2):
        x0[h].start()
        p0[h].start()
        m0[h].start()
    for copy in halo:
        copy.start()

    lane = lax.broadcasted_iota(jnp.int32, (1, HALF), 1)
    words = []
    for t in range(4):
        tile = lon * 4 + t
        word = jnp.int32(0)
        for slot in range(WIN):
            other = win_ref[slot, tile]
            place = lax.rem(lax.div(other, 4) + (LON + 1) - lon, LON) * 4 + lax.rem(other, 4)
            live = (slot < cnt_ref[tile]).astype(jnp.int32)
            word = word | lax.shift_left(live, place)
        words.append(word)
    for a in range(2):
        for n in range(3):
            for r in range(3):
                code = n * 4 + a + r
                fill = [
                    jnp.where((lax.shift_right_logical(words[2 * a + i], jnp.int32(code)) & 1) == 1, 0.0, NEG)
                    for i in range(2)
                ]
                bias[a, n * 3 + r : n * 3 + r + 1, :] = jnp.where(lane < TILE, fill[0], fill[1]).astype(F32)

    for copy in local[1:]:
        copy.wait()
    k_t[1] = k_all[1].T
    v_t[1] = v_all[1].T

    m0[0].wait_recv()
    x1[0].start()
    m1.start()
    x0[0].wait_recv()
    p2[0].start()
    m0[1].wait_recv()
    x1[1].start()
    p0[0].wait_recv()
    p0[1].wait_recv()
    p1.start()
    x0[1].wait_recv()
    p2[1].start()

    for copy in halo:
        copy.wait_recv()
    for n in (0, 2):
        k_t[n] = k_all[n].T
        v_t[n] = v_all[n].T

    def forward(h, carry):
        cols = pl.ds(pl.multiple_of(h * HEAD_DIM, HEAD_DIM), HEAD_DIM)
        for a in range(2):
            here = slice(a * HALF, (a + 1) * HALF)
            keys = slice(a * TILE, a * TILE + SPAN)
            q = q_v[here, cols]
            top = None
            for n in range(3):
                s = lax.dot_general(k_all[n, keys, cols], q, NT, preferred_element_type=F32)
                s = s.reshape(3, TILE, HALF) * (INV_ROOT * LOG2E) + bias[a, n * 3 : n * 3 + 3][:, None, :]
                s = s.reshape(SPAN, HALF)
                scores[n] = s
                peak = jnp.max(s, axis=0, keepdims=True)
                top = peak if top is None else jnp.maximum(top, peak)
            total = jnp.zeros((1, HALF), F32)
            out = jnp.zeros((HEAD_DIM, HALF), F32)
            for n in range(3):
                e = jnp.exp2(scores[n] - top)
                total += jnp.sum(e, axis=0, keepdims=True)
                low = e.astype(BF16)
                prob[h, n, a] = low
                out += dot(v_t[n, cols, keys], low)
            inverse = 1.0 / total
            inv_sum[h, :, here] = inverse
            att_t[cols, here] = (out * inverse).astype(BF16)

        @pl.when(h < 2)
        def _():
            for i in range(2):
                @pl.when(h == i)
                def _():
                    x1[i].wait_recv()
                    m2[i].start()

        return carry

    lax.fori_loop(0, HEADS_HERE, forward, 0)
    att[...] = att_t[...].T

    core_copies = []

    def use_piece(order, piece):
        block = og_t[piece]
        part = dot(w_v[:, pl.ds(pl.multiple_of(piece * COLS, COLS), COLS)], block)
        if order == 0:
            do_acc[...] = part
        else:
            do_acc[...] += part
        wg_full[...] = dot(block, att[...])
        for j in range(2):
            wg_own[piece * 2 + j] = wg_full[pl.ds(pl.multiple_of((2 * j + core) * STRIP, STRIP), STRIP)]
            core_out[piece * 2 + j] = wg_full[
                pl.ds(pl.multiple_of((2 * j + 1 - core) * STRIP, STRIP), STRIP)
            ].astype(BF16)
        both = pl.ds(piece * 2, 2)
        copy = remote(core_out.at[both], core_in.at[both], core_s.at[order], core_r.at[order], twin)
        copy.start()
        core_copies.append(copy)

    for order, piece in enumerate((tp, s_x, s_p, s_m, s_px)):
        use_piece(order, piece)
    m1.wait_recv()
    p1.wait_recv()
    use_piece(5, s_2)
    for copy in p2:
        copy.wait_recv()
    use_piece(6, s_mx)
    for copy in m2:
        copy.wait_recv()
    use_piece(7, s_2x)

    for h in range(HEADS_HERE):
        rows = slice(h * HEAD_DIM, (h + 1) * HEAD_DIM)
        scaled = (do_acc[rows] * inv_sum[h]).astype(BF16)
        do_t[rows] = scaled
        delta[h] = jnp.sum(scaled.astype(F32) * att_t[rows].astype(F32), axis=0, keepdims=True)
    do_n[...] = do_t[...].T

    for copy in core_copies:
        copy.wait_recv()

    def share(block):
        return wg_own[block] + core_in[block].astype(F32)

    up_copies, down_copies = [], []

    def ring(s):
        if s > 0:
            up_copies[s - 1].wait_recv()
            down_copies[s - 1].wait_recv()
        up_z = lax.rem(z + 4 - s, 8)
        down_z = lax.rem(z + 4 + s, 8)
        for x in range(2):
            if s > 0 or x == 0:
                value = share(x * 8 + up_z)
                if s > 1 or (s == 1 and x == 0):
                    value += up_in[s - 1, x].astype(F32)
                up_out[s, x] = value.astype(BF16)
            if s > 0 or x == 1:
                value = share(x * 8 + down_z)
                if s > 1 or (s == 1 and x == 1):
                    value += down_in[s - 1, x].astype(F32)
                down_out[s, x] = value.astype(BF16)
        if s == 0:
            up = remote(up_out.at[0, 0], up_in.at[0, 0], up_s.at[0], up_r.at[0], z_up)
            down = remote(down_out.at[0, 1], down_in.at[0, 1], down_s.at[0], down_r.at[0], z_down)
        else:
            up = remote(up_out.at[s], up_in.at[s], up_s.at[s], up_r.at[s], z_up)
            down = remote(down_out.at[s], down_in.at[s], down_s.at[s], down_r.at[s], z_down)
        up.start()
        down.start()
        up_copies.append(up)
        down_copies.append(down)

    ring(0)
    pair_copies = []

    def backward(h):
        cols = slice(h * HEAD_DIM, (h + 1) * HEAD_DIM)
        for n in (0, 2, 1):
            for a in range(2):
                here = slice(a * HALF, (a + 1) * HALF)
                keys = slice(a * TILE, a * TILE + SPAN)
                low = prob[h, n, a]
                dp = dot(v_all[n, keys, cols], do_t[cols, here])
                ds = (low.astype(F32) * (dp - delta[h, :, here])).astype(BF16)
                dkey = dot(ds, q_v[here, cols])
                dval = dot(low, do_n[here, cols])
                dquery = dot(k_t[n, cols, keys], ds)
                if n == 0:
                    dq_acc[:, here] = dquery
                else:
                    dq_acc[:, here] += dquery
                if a == 0:
                    pair_acc[0:SPAN, 0:HEAD_DIM] = dkey
                    pair_acc[0:SPAN, HEAD_DIM:] = dval
                else:
                    pair_acc[TILE:SPAN, 0:HEAD_DIM] += dkey[:HALF]
                    pair_acc[TILE:SPAN, HEAD_DIM:] += dval[:HALF]
                    pair_acc[SPAN:, 0:HEAD_DIM] = dkey[HALF:]
                    pair_acc[SPAN:, HEAD_DIM:] = dval[HALF:]
            if n == 1:
                own_pair[h] = pair_acc[...]
            else:
                way = n // 2
                pair_out[way, h] = pair_acc[...].astype(BF16)
                number = h * 2 + way
                copy = remote(
                    pair_out.at[way, h], pair_in.at[way, h], pair_s.at[number], pair_r.at[number],
                    right if way else left,
                )
                copy.start()
                pair_copies.append(copy)
        dq_ref[:, cols] = (dq_acc[...] * INV_ROOT).astype(BF16).T

    for h in range(HEADS_HERE):
        backward(h)
        ring(h + 1)

    up_copies[3].wait_recv()
    down_copies[3].wait_recv()

    def gathered(x):
        return share(x * 8 + z) + up_in[3, x].astype(F32) + down_in[3, x].astype(F32)

    x_out[...] = gathered(1 - x_hi).astype(BF16)
    swap = remote(x_out, x_in, x_s.at[0], x_r.at[0], x_far)
    swap.start()

    for h in range(HEADS_HERE):
        cols = slice(h * HEAD_DIM, (h + 1) * HEAD_DIM)
        pair_copies[2 * h].wait_recv()
        pair_copies[2 * h + 1].wait_recv()
        total = own_pair[h] + pair_in[0, h].astype(F32) + pair_in[1, h].astype(F32)
        dk_ref[:, cols] = (total[:, :HEAD_DIM] * INV_ROOT).astype(BF16)
        dv_ref[:, cols] = total[:, HEAD_DIM:].astype(BF16)

    swap.wait_recv()
    wg_ref[...] = (gathered(x_hi) + x_in[...].astype(F32)).astype(BF16)

    for copy in (*x0, *p0, *m0, *x1, m1, p1, *p2, *m2, *halo, *core_copies, *up_copies, *down_copies, *pair_copies, swap):
        copy.wait_send()


def body(queries, keys, values, out_grad, out_weight, window, counts):
    hbm = pl.BlockSpec(memory_space=pl.ANY)
    vmem = pl.BlockSpec(memory_space=pltpu.VMEM)
    smem = pl.BlockSpec(memory_space=pltpu.SMEM)
    V = pltpu.VMEM
    dma = pltpu.SemaphoreType.DMA
    block = jax.ShapeDtypeStruct((TOK, COLS), BF16)
    scratch = [
        V((TOK, COLS), BF16),
        V((3, TOK, COLS), BF16),
        V((3, TOK, COLS), BF16),
        V((TOK, COLS), BF16),
        V((COLS, TP * COLS), BF16),
        V((TP, COLS, TOK), BF16),
        V((3, COLS, TOK), BF16),
        V((3, COLS, TOK), BF16),
        V((HEADS_HERE, 3, 2, SPAN, HALF), BF16),
        V((3, SPAN, HALF), F32),
        V((2, 16, HALF), F32),
        V((COLS, TOK), BF16),
        V((TOK, COLS), BF16),
        V((HEADS_HERE, 1, TOK), F32),
        V((HEADS_HERE, 1, TOK), F32),
        V((COLS, TOK), F32),
        V((COLS, TOK), BF16),
        V((TOK, COLS), BF16),
        V((HEAD_DIM, TOK), F32),
        V((TOK, HALF), F32),
        V((HEADS_HERE, TOK, HALF), F32),
        V((2, HEADS_HERE, TOK, HALF), BF16),
        V((2, HEADS_HERE, TOK, HALF), BF16),
        V((COLS, COLS), F32),
        V((16, STRIP, COLS), F32),
        V((16, STRIP, COLS), BF16),
        V((16, STRIP, COLS), BF16),
        V((4, 2, STRIP, COLS), BF16),
        V((4, 2, STRIP, COLS), BF16),
        V((4, 2, STRIP, COLS), BF16),
        V((4, 2, STRIP, COLS), BF16),
        V((STRIP, COLS), BF16),
        V((STRIP, COLS), BF16),
        dma((5,)),
        dma((4,)), dma((4,)),
        dma((14,)), dma((14,)),
        dma((6,)), dma((6,)),
        dma((8,)), dma((8,)),
        dma((4,)), dma((4,)),
        dma((4,)), dma((4,)),
        dma((1,)), dma((1,)),
    ]
    dq, dk, dv, wg = pl.pallas_call(
        kernel,
        out_shape=(block, block, block, jax.ShapeDtypeStruct((STRIP, COLS), BF16)),
        in_specs=[smem, smem, hbm, hbm, hbm, hbm, hbm],
        out_specs=(vmem, vmem, vmem, vmem),
        scratch_shapes=scratch,
        compiler_params=pltpu.CompilerParams(
            collective_id=0, has_side_effects=True, vmem_limit_bytes=56 * 1024 * 1024
        ),
    )(window.T, counts, queries, keys, values, out_grad, out_weight)
    return dq, dk, dv, wg.T


def solution(mesh):
    in_specs = (
        P("lon", "tp"),
        P("lon", "tp"),
        P("lon", "tp"),
        P("lon", "tp"),
        P("tp", None),
        P(),
        P(),
    )
    out_specs = (P("lon", "tp"), P("lon", "tp"), P("lon", "tp"), P("tp", "lon"))
    return jax.shard_map(body, mesh=mesh, in_specs=in_specs, out_specs=out_specs, check_vma=False)
```

time: 238 us -> 79.6 us (0.33); the launches traced: 235 us -> 79.4 us
  waiting for transfers between devices: 171 us -> 0 us
  Pallas kernels: 0 us -> 72.7 us
  matrix products: 22.1 us -> 0 us
  between operations: 14.4 us -> 0.65 us
  other arithmetic: 11 us -> 0 us
  local copies, waits for them, and re-layouts: 12.3 us -> 6.01 us
  starting transfers between devices: 3.91 us -> 0 us
    reduce_scatter x1 -> x0, waiting for transfers between devices: 84.1 us -> none  [body(): lax.psum_scatter(column_store, 'lon', scatter_dimension=1, tiled=True)]
    pallas_call x0 -> x1, Pallas kernels: none -> 72.7 us  [body(): pl.pallas_call(kernel, out_shape=(block, block, block, jax.ShapeDtypeStru...]
    all_gather x1 -> x0, waiting for transfers between devices: 61.6 us -> none  [body(): piece = lax.all_gather(out_grad, 'tp', axis=1, tiled=True)]
    ppermute x4 -> x0, waiting for transfers between devices: 24.6 us -> none  [the longest x2 17.7 us: passed_along(): return lax.ppermute(block, axis, route)]
    dot_general x20 -> x0, matrix products: 22.1 us -> none  [the longest x3 4.7 us: body(): jnp.einsum('qd,kd->qk', grad_here, near_values[:, columns], preferred_ele...]
    convert_element_type x4 -> x0, other arithmetic: 4.19 us -> none  [the longest x3 2.64 us: body(): probs_low = probs.astype(jnp.bfloat16)]
    ppermute x4 -> x0, starting transfers between devices: 3.83 us -> none  [the longest x1 3.32 us: extended(): after = lax.ppermute(leading, axis, down)]
    another operation x1 -> x0, other arithmetic: 2.9 us -> none
  transfers between devices with their start and end apart: 6 -> 0, of which waited for: 5 -> 0; matrix products, arithmetic and copies ran while one was open for 13% -> 0% of each run, Pallas kernels for 0% -> 0%
where the time goes in v1:
time: 79.6 us; the launch traced here: 79.4 us
  Pallas kernels  72.7 us (91%)
  local copies, waits for them, and re-layouts  6.01 us (8%)
    pallas_call x1, Pallas kernels, body(): pl.pallas_call(kernel, out_shape=(block, block, block, jax.ShapeDtypeStru...  72.7 us
    unnamed x6, local copies, waits for them, and re-layouts  6.01 us

profile of v1, /device:TPU:1, one launch (start us, length us, event | category | flops | bytes accessed | tf_op | source)
XLA Modules:
  0.0 79.4 jit_solution(8257821231163027423)
XLA Ops:
  0.6 72.7 %shard_map.102 = (bf16[512,384]{1,0:T(8,128)(2,1)}, bf16[512,384]{1,0:T(8,128)(2,1)}, bf16[512,384]{1,0:T(8,128)(2,1)}, bf16[96,384]{1,0:T(8,128)(2,1)}) custom-call(s32[9,128]{1,0:T(8,128)} %bitcast.3, s32[128]{0:T(128)} %cnt_ref.1, bf16[512,384]{1,0:T(8,128)(2,1)} %q_hbm.1, bf16[512,384]{1,0:T(8,128)(2,1)} %k_hbm.1, bf16[512,384]{1,0:T(8,128)(2,1)} %v_hbm.1, ...), custom_call_target="tpu_custom_call" | custom-call | tf_op jit(solution)/shard_map/pallas_call | solution.py:394
  73.3 0.0 copy-start
  73.3 1.8 %copy.15 = bf16[512,384]{1,0:T(8,128)(2,1)} copy(bf16[512,384]{1,0:T(8,128)(2,1)} %get-tuple-element.16) | data formatting | bytes 786432
  75.2 1.8 %copy.16 = bf16[512,384]{1,0:T(8,128)(2,1)} copy(bf16[512,384]{1,0:T(8,128)(2,1)} %get-tuple-element.17) | data formatting | bytes 786432
  76.9 1.8 %copy.17 = bf16[512,384]{1,0:T(8,128)(2,1)} copy(bf16[512,384]{1,0:T(8,128)(2,1)} %get-tuple-element.18) | data formatting | bytes 786432
  78.7 0.0 copy-done
  78.7 0.6 copy.18
Async XLA Ops:
  73.3 5.4 %copy-start = (bf16[96,384]{1,0:T(8,128)(2,1)S(1)}, bf16[96,384]{1,0:T(8,128)(2,1)}, u32[]{:S(2)}) copy-start(bf16[96,384]{1,0:T(8,128)(2,1)} %get-tuple-element.11) | copy-start | bytes 221188

commit v2 on v1

v2 whole, which is shorter than its diff:
```python
import jax
import jax.numpy as jnp
from jax import lax
from jax.experimental import pallas as pl
from jax.experimental.pallas import tpu as pltpu
from jax.sharding import PartitionSpec as P

MESH = pl.DeviceIdType.MESH
F32 = jnp.float32
BF16 = jnp.bfloat16
HEAD_DIM = 128
TILE = 128
HEADS_HERE = 3
TOK = 512
COLS = HEADS_HERE * HEAD_DIM
SPAN = 3 * TILE
HALF = 2 * TILE
WIN = 9
LON = 32
TP = 8
STRIP = 96
GATHERS = 28
INV_ROOT = HEAD_DIM ** -0.5
LOG2E = 1.4426950408889634
NEG = -1e30

NT = (((1,), (1,)), ((), ()))


def dot(a, b):
    return jnp.dot(a, b, preferred_element_type=F32)


def kernel(
    win_ref, cnt_ref, q_hbm, k_hbm, v_hbm, og_hbm, w_hbm,
    dq_ref, dk_ref, dv_ref, wg_ref,
    q_v, k_all, v_all, og_v, w_v, og_t, k_t, v_t, prob, scores, bias,
    att_t, att, inv_sum, delta, do_acc, do_t, do_n, dq_acc, pair_acc,
    own_pair, pair_out, pair_in, wg_full, wg_own, core_out, core_in,
    ring_out, ring_in, x_out, x_in,
    loc_sem, halo_s, halo_r, ag_s, ag_r, pair_s, pair_r, core_s, core_r,
    ring_s, ring_r, x_s, x_r,
):
    lon = lax.axis_index("lon")
    tp = lax.axis_index("tp")
    x_hi = lax.div(lon, 16)
    z = lax.rem(lax.div(lon, 2), 8)
    core = lax.rem(lon, 2)
    y = lax.div(tp, 2)
    x_lo = lax.rem(tp, 2)

    right = {"lon": lax.rem(lon + 1, LON)}
    left = {"lon": lax.rem(lon + LON - 1, LON)}
    twin = {"lon": lon + 1 - 2 * core}
    z_up = {"lon": x_hi * 16 + lax.rem(z + 1, 8) * 2 + core}
    z_down = {"lon": x_hi * 16 + lax.rem(z + 7, 8) * 2 + core}
    x_far = {"lon": lax.rem(lon + 16, LON)}
    up_far = {"lon": (1 - x_hi) * 16 + lax.rem(z + 1, 8) * 2 + core}
    down_far = {"lon": (1 - x_hi) * 16 + lax.rem(z + 7, 8) * 2 + core}
    y_p = lax.rem(y + 1, 4)
    y_m = lax.rem(y + 3, 4)
    y_2 = lax.rem(y + 2, 4)
    s_x = y * 2 + 1 - x_lo
    s_p = y_p * 2 + x_lo
    s_m = y_m * 2 + x_lo
    s_2 = y_2 * 2 + x_lo
    s_px = y_p * 2 + 1 - x_lo
    s_mx = y_m * 2 + 1 - x_lo
    s_2x = y_2 * 2 + 1 - x_lo
    to_x, to_p, to_m = {"tp": s_x}, {"tp": s_p}, {"tp": s_m}

    barrier = pltpu.get_barrier_semaphore()
    for other in (right, left, z_up, z_down, x_far, up_far, down_far, to_x, to_p, to_m):
        pl.semaphore_signal(barrier, inc=1, device_id=other, device_id_type=MESH)

    def head(h):
        return slice(h * HEAD_DIM, (h + 1) * HEAD_DIM)

    local_og = pltpu.make_async_copy(og_hbm, og_v, loc_sem.at[0])
    local_kv = [
        pltpu.make_async_copy(src.at[:, head(h)], dst.at[1, h], loc_sem.at[1 + 2 * h + i])
        for h in range(HEADS_HERE)
        for i, (src, dst) in enumerate(((k_hbm, k_all), (v_hbm, v_all)))
    ]
    local_q = pltpu.make_async_copy(q_hbm, q_v, loc_sem.at[7])
    local_w = pltpu.make_async_copy(w_hbm, w_v, loc_sem.at[8])
    for copy in (local_og, *local_kv, local_q, local_w):
        copy.start()

    sent = []

    def remote(src, dst, send, recv, to):
        copy = pltpu.make_async_remote_copy(
            src_ref=src, dst_ref=dst, send_sem=send, recv_sem=recv, device_id=to, device_id_type=MESH
        )
        sent.append(copy)
        return copy

    count = iter(range(GATHERS))

    def gather(slot, quarter, to):
        block = og_t.at[slot, pl.ds(quarter * STRIP, STRIP)]
        number = next(count)
        return remote(block, block, ag_s.at[number], ag_r.at[number], to)

    x0 = {i: gather(tp, i, to_x) for i in (0, 1, 2, 3)}
    p0 = {i: gather(tp, i, to_p) for i in (2, 3, 0, 1)}
    m0 = {i: gather(tp, i, to_m) for i in (0, 1, 2, 3)}
    p1 = {i: gather(s_m, i, to_p) for i in (2, 3)}
    m1 = {i: gather(s_p, i, to_m) for i in (0, 1)}
    p2 = {i: gather(s_x, i, to_p) for i in (2, 3, 1)}
    m2 = {i: gather(s_x, i, to_m) for i in (0, 1, 2)}
    x1 = {3: gather(s_p, 3, to_x)}
    x2 = {0: gather(s_m, 0, to_x)}
    p3 = {i: gather(s_mx, i, to_p) for i in (2, 3)}
    m3 = {i: gather(s_px, i, to_m) for i in (0, 1)}

    halo = []
    for h in range(HEADS_HERE):
        part = []
        for i, ref in enumerate((k_all, v_all)):
            for j, to in enumerate((right, left)):
                number = h * 4 + i * 2 + j
                part.append(
                    remote(ref.at[1, h], ref.at[2 * j, h], halo_s.at[number], halo_r.at[number], to)
                )
        halo.append(part)

    local_og.wait()
    og_t[tp] = og_v[...].T
    for copy in (*local_kv, local_q):
        copy.wait()
    pl.semaphore_wait(barrier, 10)
    for i, (a, b, c) in enumerate(zip(x0.values(), p0.values(), m0.values(), strict=True)):
        a.start()
        b.start()
        c.start()

    around = (lax.rem(lon, 16) == 15, lax.rem(lon, 16) == 0)

    def send_halo(late):
        for j in range(2):
            @pl.when(around[j] if late else jnp.logical_not(around[j]))
            def _():
                for h in range(HEADS_HERE):
                    halo[h][j].start()
                    halo[h][2 + j].start()

    send_halo(False)

    lane = lax.broadcasted_iota(jnp.int32, (1, HALF), 1)
    words = []
    for t in range(4):
        tile = lon * 4 + t
        word = jnp.int32(0)
        for slot in range(WIN):
            other = win_ref[slot, tile]
            place = lax.rem(lax.div(other, 4) + (LON + 1) - lon, LON) * 4 + lax.rem(other, 4)
            live = (slot < cnt_ref[tile]).astype(jnp.int32)
            word = word | lax.shift_left(live, place)
        words.append(word)
    for a in range(2):
        for n in range(3):
            for r in range(3):
                code = n * 4 + a + r
                fill = [
                    jnp.where((lax.shift_right_logical(words[2 * a + i], jnp.int32(code)) & 1) == 1, 0.0, NEG)
                    for i in range(2)
                ]
                bias[a, n * 3 + r : n * 3 + r + 1, :] = jnp.where(lane < TILE, fill[0], fill[1]).astype(F32)

    for h in range(HEADS_HERE):
        k_t[1, h] = k_all[1, h].T
        v_t[1, h] = v_all[1, h].T

    def forward(h, a):
        cols = head(h)
        here = slice(a * HALF, (a + 1) * HALF)
        keys = slice(a * TILE, a * TILE + SPAN)
        q = q_v[here, cols]
        top = None
        for n in range(3):
            s = lax.dot_general(k_all[n, h, keys, :], q, NT, preferred_element_type=F32)
            s = s.reshape(3, TILE, HALF) * (INV_ROOT * LOG2E) + bias[a, n * 3 : n * 3 + 3][:, None, :]
            s = s.reshape(SPAN, HALF)
            scores[n] = s
            peak = jnp.max(s, axis=0, keepdims=True)
            top = peak if top is None else jnp.maximum(top, peak)
        total = jnp.zeros((1, HALF), F32)
        out = jnp.zeros((HEAD_DIM, HALF), F32)
        for n in range(3):
            e = jnp.exp2(scores[n] - top)
            total += jnp.sum(e, axis=0, keepdims=True)
            low = e.astype(BF16)
            prob[h, n, a] = low
            out += dot(v_t[n, h, :, keys], low)
        inverse = 1.0 / total
        inv_sum[h, :, here] = inverse
        att_t[cols, here] = (out * inverse).astype(BF16)

    def passed(before, after):
        for copy in before:
            copy.wait_recv()
        for copy in after:
            copy.start()

    passed((p0[2], p0[3], m0[0], m0[1]), (*p1.values(), *m1.values()))
    passed((x0[0], x0[1], x0[2]), (p2[2], m2[0], m2[1], p2[1]))
    passed((x0[3],), (p2[3], m2[2]))
    send_halo(True)
    passed((m0[2], m0[3], p0[0], p0[1]), (x1[3], x2[0]))

    for h in range(HEADS_HERE):
        for copy in halo[h]:
            copy.wait_recv()
        for n in (0, 2):
            v_t[n, h] = v_all[n, h].T
        forward(h, 0)
        forward(h, 1)
    passed((p2[2], m2[0]), (p3[2], m3[0]))
    passed((p2[3], m2[1]), (p3[3], m3[1]))
    att[...] = att_t[...].T
    for h in range(HEADS_HERE):
        for n in (0, 2):
            k_t[n, h] = k_all[n, h].T

    core_copies = []

    def use_piece(order, piece):
        block = og_t[piece]
        part = dot(w_v[:, pl.ds(pl.multiple_of(piece * COLS, COLS), COLS)], block)
        if order == 0:
            do_acc[...] = part
        else:
            do_acc[...] += part
        wg_full[...] = dot(block, att[...])
        for j in range(2):
            wg_own[piece * 2 + j] = wg_full[pl.ds(pl.multiple_of((2 * j + core) * STRIP, STRIP), STRIP)]
            core_out[piece * 2 + j] = wg_full[
                pl.ds(pl.multiple_of((2 * j + 1 - core) * STRIP, STRIP), STRIP)
            ].astype(BF16)
        both = pl.ds(piece * 2, 2)
        copy = remote(core_out.at[both], core_in.at[both], core_s.at[order], core_r.at[order], twin)
        copy.start()
        core_copies.append(copy)

    local_w.wait()
    use_piece(0, tp)
    use_piece(1, s_x)
    use_piece(2, s_p)
    use_piece(3, s_m)
    passed((*p1.values(), *m1.values()), ())
    use_piece(4, s_2)
    passed((x1[3], m2[2]), ())
    use_piece(5, s_px)
    passed((x2[0], p2[1]), ())
    use_piece(6, s_mx)
    passed((*p3.values(), *m3.values()), ())
    use_piece(7, s_2x)

    for h in range(HEADS_HERE):
        rows = head(h)
        scaled = (do_acc[rows] * inv_sum[h]).astype(BF16)
        do_t[rows] = scaled
        delta[h] = jnp.sum(scaled.astype(F32) * att_t[rows].astype(F32), axis=0, keepdims=True)
    do_n[...] = do_t[...].T

    for copy in core_copies:
        copy.wait_recv()

    def share(block):
        return wg_own[block] + core_in[block].astype(F32)

    chains = {}

    def chain(way, x, s):
        first = s == (0 if way == x else 1)
        step = lax.rem(z + (4 - s if way == 0 else 4 + s), 8)
        value = share(x * 8 + step)
        if not first:
            chains[way, x, s - 1].wait_recv()
            value += ring_in[way, x, s - 1].astype(F32)
        ring_out[way, x, s] = value.astype(BF16)
        number = way * 8 + x * 4 + s
        if s < 3:
            copy = remote(
                ring_out.at[way, x, s], ring_in.at[way, x, s], ring_s.at[number], ring_r.at[number],
                z_down if way else z_up,
            )
        else:
            copy = remote(
                ring_out.at[way, x, s], ring_in.at[way, x_hi, s], ring_s.at[number], ring_r.at[way * 8 + x_hi * 4 + s],
                {"lon": x * 16 + lax.rem(z + (7 if way else 1), 8) * 2 + core},
            )
        copy.start()
        chains[way, x, s] = copy

    def ring(point):
        chain(0, 0, point)
        chain(1, 1, point)
        if point < 3:
            chain(0, 1, point + 1)
            chain(1, 0, point + 1)

    pair_copies = {}

    def backward(h, n):
        cols = head(h)
        for a in range(2):
            here = slice(a * HALF, (a + 1) * HALF)
            keys = slice(a * TILE, a * TILE + SPAN)
            low = prob[h, n, a]
            dp = dot(v_all[n, h, keys, :], do_t[cols, here])
            ds = (low.astype(F32) * (dp - delta[h, :, here])).astype(BF16)
            dkey = dot(ds, q_v[here, cols])
            dval = dot(low, do_n[here, cols])
            dquery = dot(k_t[n, h, :, keys], ds)
            if n == 0:
                dq_acc[h, :, here] = dquery
            else:
                dq_acc[h, :, here] += dquery
            if a == 0:
                pair_acc[0:SPAN, 0:HEAD_DIM] = dkey
                pair_acc[0:SPAN, HEAD_DIM:] = dval
            else:
                pair_acc[TILE:SPAN, 0:HEAD_DIM] += dkey[:HALF]
                pair_acc[TILE:SPAN, HEAD_DIM:] += dval[:HALF]
                pair_acc[SPAN:, 0:HEAD_DIM] = dkey[HALF:]
                pair_acc[SPAN:, HEAD_DIM:] = dval[HALF:]
        if n == 1:
            own_pair[h] = pair_acc[...]
        else:
            way = n // 2
            pair_out[way, h] = pair_acc[...].astype(BF16)
            number = h * 2 + way
            copy = remote(
                pair_out.at[way, h], pair_in.at[way, h], pair_s.at[number], pair_r.at[number],
                right if way else left,
            )
            copy.start()
            pair_copies[h, way] = copy

    ring(0)
    x_out[...] = share((1 - x_hi) * 8 + z).astype(BF16)
    swap = remote(x_out, x_in, x_s.at[0], x_r.at[0], x_far)
    swap.start()
    backward(0, 0)
    backward(0, 2)
    ring(1)
    backward(1, 0)
    backward(1, 2)
    ring(2)
    backward(2, 0)
    backward(2, 2)
    ring(3)
    for h in range(HEADS_HERE):
        backward(h, 1)
        dq_ref[:, head(h)] = (dq_acc[h] * INV_ROOT).astype(BF16).T

    for h in range(HEADS_HERE):
        cols = head(h)
        for way in range(2):
            pair_copies[h, way].wait_recv()
        total = own_pair[h] + pair_in[0, h].astype(F32) + pair_in[1, h].astype(F32)
        dk_ref[:, cols] = (total[:, :HEAD_DIM] * INV_ROOT).astype(BF16)
        dv_ref[:, cols] = total[:, HEAD_DIM:].astype(BF16)

    swap.wait_recv()
    total = share(x_hi * 8 + z) + x_in[...].astype(F32)
    for way in range(2):
        for x in range(2):
            number = way * 8 + x * 4 + 3
            pltpu.make_async_copy(ring_out.at[way, x, 3], ring_in.at[way, x, 3], ring_r.at[number]).wait()
            total += ring_in[way, x, 3].astype(F32)
    wg_ref[...] = total.astype(BF16)

    for copy in sent:
        copy.wait_send()


def copy_out(*refs):
    given, out, kept, sem = refs[:4], refs[4:8], refs[8:12], refs[12]
    reads = [pltpu.make_async_copy(given[i], kept[i], sem.at[i]) for i in range(4)]
    writes = [pltpu.make_async_copy(kept[i], out[i], sem.at[4 + i]) for i in range(4)]
    for copy in reads:
        copy.start()
    for read, write in zip(reads, writes, strict=True):
        read.wait()
        write.start()
    for copy in writes:
        copy.wait()


def body(queries, keys, values, out_grad, out_weight, window, counts):
    hbm = pl.BlockSpec(memory_space=pl.ANY)
    vmem = pl.BlockSpec(memory_space=pltpu.VMEM)
    smem = pl.BlockSpec(memory_space=pltpu.SMEM)
    V = pltpu.VMEM
    dma = pltpu.SemaphoreType.DMA
    block = jax.ShapeDtypeStruct((TOK, COLS), BF16)
    scratch = [
        V((TOK, COLS), BF16),
        V((3, HEADS_HERE, TOK, HEAD_DIM), BF16),
        V((3, HEADS_HERE, TOK, HEAD_DIM), BF16),
        V((TOK, COLS), BF16),
        V((COLS, TP * COLS), BF16),
        V((TP, COLS, TOK), BF16),
        V((3, HEADS_HERE, HEAD_DIM, TOK), BF16),
        V((3, HEADS_HERE, HEAD_DIM, TOK), BF16),
        V((HEADS_HERE, 3, 2, SPAN, HALF), BF16),
        V((3, SPAN, HALF), F32),
        V((2, 16, HALF), F32),
        V((COLS, TOK), BF16),
        V((TOK, COLS), BF16),
        V((HEADS_HERE, 1, TOK), F32),
        V((HEADS_HERE, 1, TOK), F32),
        V((COLS, TOK), F32),
        V((COLS, TOK), BF16),
        V((TOK, COLS), BF16),
        V((HEADS_HERE, HEAD_DIM, TOK), F32),
        V((TOK, HALF), F32),
        V((HEADS_HERE, TOK, HALF), F32),
        V((2, HEADS_HERE, TOK, HALF), BF16),
        V((2, HEADS_HERE, TOK, HALF), BF16),
        V((COLS, COLS), F32),
        V((16, STRIP, COLS), F32),
        V((16, STRIP, COLS), BF16),
        V((16, STRIP, COLS), BF16),
        V((2, 2, 4, STRIP, COLS), BF16),
        V((2, 2, 4, STRIP, COLS), BF16),
        V((STRIP, COLS), BF16),
        V((STRIP, COLS), BF16),
        dma((9,)),
        dma((12,)), dma((12,)),
        dma((GATHERS,)), dma((GATHERS,)),
        dma((6,)), dma((6,)),
        dma((8,)), dma((8,)),
        dma((16,)), dma((16,)),
        dma((1,)), dma((1,)),
    ]
    dq, dk, dv, wg = pl.pallas_call(
        kernel,
        out_shape=(block, block, block, jax.ShapeDtypeStruct((STRIP, COLS), BF16)),
        in_specs=[smem, smem, hbm, hbm, hbm, hbm, hbm],
        out_specs=(vmem, vmem, vmem, vmem),
        scratch_shapes=scratch,
        compiler_params=pltpu.CompilerParams(
            collective_id=0, has_side_effects=True, vmem_limit_bytes=56 * 1024 * 1024
        ),
    )(window.T, counts, queries, keys, values, out_grad, out_weight)
    results = (dq, dk, dv, wg)
    dq, dk, dv, wg = pl.pallas_call(
        copy_out,
        out_shape=tuple(jax.ShapeDtypeStruct(r.shape, BF16) for r in results),
        in_specs=[hbm] * 4,
        out_specs=(hbm,) * 4,
        scratch_shapes=[V(r.shape, BF16) for r in results] + [dma((8,))],
    )(*results)
    return dq, dk, dv, wg.T


def solution(mesh):
    in_specs = (
        P("lon", "tp"),
        P("lon", "tp"),
        P("lon", "tp"),
        P("lon", "tp"),
        P("tp", None),
        P(),
        P(),
    )
    out_specs = (P("lon", "tp"), P("lon", "tp"), P("lon", "tp"), P("tp", "lon"))
    return jax.shard_map(body, mesh=mesh, in_specs=in_specs, out_specs=out_specs, check_vma=False)
```

time: 79.6 us -> 69.3 us (0.87)
  local copies, waits for them, and re-layouts: 6.01 us -> 0 us
  Pallas kernels: 72.7 us -> 68.5 us
    pallas_call x1, Pallas kernels: 72.7 us -> 66.4 us  [body(): pl.pallas_call(kernel, out_shape=(block, block, block, jax.ShapeDtypeStru...]
    unnamed x6 -> x0, local copies, waits for them, and re-layouts: 6.01 us -> none
    pallas_call x0 -> x1, Pallas kernels: none -> 2.09 us  [body(): pl.pallas_call(copy_out, out_shape=tuple((jax.ShapeDtypeStruct(r.shape, B...]
where the time goes in v2:
time: 69.3 us; the launch traced here: 69.1 us
  Pallas kernels  68.5 us (99%)
    pallas_call x1, Pallas kernels, body(): pl.pallas_call(kernel, out_shape=(block, block, block, jax.ShapeDtypeStru...  66.4 us
    pallas_call x1, Pallas kernels, body(): pl.pallas_call(copy_out, out_shape=tuple((jax.ShapeDtypeStruct(r.shape, B...  2.09 us

profile of v2, /device:TPU:1, one launch (start us, length us, event | category | flops | bytes accessed | tf_op | source)
XLA Modules:
  0.0 69.1 jit_solution(13249934547644815918)
XLA Ops:
  0.6 66.4 %shard_map.102 = (bf16[512,384]{1,0:T(8,128)(2,1)}, bf16[512,384]{1,0:T(8,128)(2,1)}, bf16[512,384]{1,0:T(8,128)(2,1)}, bf16[96,384]{1,0:T(8,128)(2,1)}) custom-call(s32[9,128]{1,0:T(8,128)} %bitcast.2, s32[128]{0:T(128)} %cnt_ref.1, bf16[512,384]{1,0:T(8,128)(2,1)} %q_hbm.1, bf16[512,384]{1,0:T(8,128)(2,1)} %k_hbm.1, bf16[512,384]{1,0:T(8,128)(2,1)} %v_hbm.1, ...), custom_call_target="tpu_custom_call" | custom-call | tf_op jit(solution)/shard_map/pallas_call | solution.py:441
  67.0 2.1 %shard_map.103 = (bf16[512,384]{1,0:T(8,128)(2,1)}, bf16[512,384]{1,0:T(8,128)(2,1)}, bf16[512,384]{1,0:T(8,128)(2,1)}, bf16[96,384]{1,0:T(8,128)(2,1)}) custom-call(bf16[512,384]{1,0:T(8,128)(2,1)} %get-tuple-element.12.refs_0_, bf16[512,384]{1,0:T(8,128)(2,1)} %get-tuple-element.13.refs_1_, bf16[512,384]{1,0:T(8,128)(2,1)} %get-tuple-element.14.refs_2_, ...), custom_call_target="tpu_custom_call" | custom-call | tf_op jit(solution)/shard_map/pallas_call | solution.py:452

commit v3 on v2

--- a/solution.py
+++ b/solution.py
@@ -34,12 +34,12 @@
 def kernel(
     win_ref, cnt_ref, q_hbm, k_hbm, v_hbm, og_hbm, w_hbm,
     dq_ref, dk_ref, dv_ref, wg_ref,
-    q_v, k_all, v_all, og_v, w_v, og_t, k_t, v_t, prob, scores, bias,
-    att_t, att, inv_sum, delta, do_acc, do_t, do_n, dq_acc, pair_acc,
-    own_pair, pair_out, pair_in, wg_full, wg_own, core_out, core_in,
-    ring_out, ring_in, x_out, x_in,
-    loc_sem, halo_s, halo_r, ag_s, ag_r, pair_s, pair_r, core_s, core_r,
-    ring_s, ring_r, x_s, x_r,
+    q_all, k_all, v_all, og_v, w_v, og_t, k_t, v_t, prob, prob_near, scores, bias, bias_near, top_all,
+    att_t, att, inv_sum, delta, do_acc, do_all, pair,
+    wg_full, wg_own, core_out, core_in,
+    ring_out, ring_in, last_in, x_out, x_in,
+    loc_sem, halo_s, halo_r, ag_s, ag_r, ask_s, ask_r, stat_s, stat_r, tell_s, tell_r, core_s, core_r,
+    ring_s, ring_r, last_r, x_s, x_r,
 ):
     lon = lax.axis_index("lon")
     tp = lax.axis_index("tp")
@@ -54,6 +54,8 @@
     twin = {"lon": lon + 1 - 2 * core}
     z_up = {"lon": x_hi * 16 + lax.rem(z + 1, 8) * 2 + core}
     z_down = {"lon": x_hi * 16 + lax.rem(z + 7, 8) * 2 + core}
+    z_up2 = {"lon": x_hi * 16 + lax.rem(z + 2, 8) * 2 + core}
+    z_down2 = {"lon": x_hi * 16 + lax.rem(z + 6, 8) * 2 + core}
     x_far = {"lon": lax.rem(lon + 16, LON)}
     up_far = {"lon": (1 - x_hi) * 16 + lax.rem(z + 1, 8) * 2 + core}
     down_far = {"lon": (1 - x_hi) * 16 + lax.rem(z + 7, 8) * 2 + core}
@@ -70,7 +72,7 @@
     to_x, to_p, to_m = {"tp": s_x}, {"tp": s_p}, {"tp": s_m}
 
     barrier = pltpu.get_barrier_semaphore()
-    for other in (right, left, z_up, z_down, x_far, up_far, down_far, to_x, to_p, to_m):
+    for other in (right, left, z_up, z_down, z_up2, z_down2, x_far, up_far, down_far, to_x, to_p, to_m):
         pl.semaphore_signal(barrier, inc=1, device_id=other, device_id_type=MESH)
 
     def head(h):
@@ -78,13 +80,12 @@
 
     local_og = pltpu.make_async_copy(og_hbm, og_v, loc_sem.at[0])
     local_kv = [
-        pltpu.make_async_copy(src.at[:, head(h)], dst.at[1, h], loc_sem.at[1 + 2 * h + i])
+        pltpu.make_async_copy(src.at[:, head(h)], dst.at[1, h], loc_sem.at[1 + 3 * h + i])
         for h in range(HEADS_HERE)
-        for i, (src, dst) in enumerate(((k_hbm, k_all), (v_hbm, v_all)))
+        for i, (src, dst) in enumerate(((k_hbm, k_all), (v_hbm, v_all), (q_hbm, q_all)))
     ]
-    local_q = pltpu.make_async_copy(q_hbm, q_v, loc_sem.at[7])
-    local_w = pltpu.make_async_copy(w_hbm, w_v, loc_sem.at[8])
-    for copy in (local_og, *local_kv, local_q, local_w):
+    local_w = pltpu.make_async_copy(w_hbm, w_v, loc_sem.at[10])
+    for copy in (local_og, *local_kv, local_w):
         copy.start()
 
     sent = []
@@ -125,12 +126,17 @@
                     remote(ref.at[1, h], ref.at[2 * j, h], halo_s.at[number], halo_r.at[number], to)
                 )
         halo.append(part)
+    ways = (right, left)
+    ask = [
+        [remote(q_all.at[1, h], q_all.at[2 * j, h], ask_s.at[2 * h + j], ask_r.at[2 * h + j], ways[j]) for j in range(2)]
+        for h in range(HEADS_HERE)
+    ]
 
     local_og.wait()
     og_t[tp] = og_v[...].T
-    for copy in (*local_kv, local_q):
+    for copy in local_kv:
         copy.wait()
-    pl.semaphore_wait(barrier, 10)
+    pl.semaphore_wait(barrier, 12)
     for i, (a, b, c) in enumerate(zip(x0.values(), p0.values(), m0.values(), strict=True)):
         a.start()
         b.start()
@@ -145,6 +151,8 @@
                 for h in range(HEADS_HERE):
                     halo[h][j].start()
                     halo[h][2 + j].start()
+                for h in range(HEADS_HERE):
+                    ask[h][j].start()
 
     send_halo(False)
 
@@ -169,6 +177,24 @@
                 ]
                 bias[a, n * 3 + r : n * 3 + r + 1, :] = jnp.where(lane < TILE, fill[0], fill[1]).astype(F32)
 
+    for i, stripe in enumerate((lax.rem(lon + LON - 1, LON), lax.rem(lon + 1, LON))):
+        words = []
+        for t in range(4):
+            tile = stripe * 4 + t
+            word = jnp.int32(0)
+            for slot in range(WIN):
+                other = win_ref[slot, tile]
+                live = ((slot < cnt_ref[tile]) & (lax.div(other, 4) == lon)).astype(jnp.int32)
+                word = word | lax.shift_left(live, lax.rem(other, 4))
+            words.append(word)
+        for a in range(2):
+            for r in range(3):
+                fill = [
+                    jnp.where((lax.shift_right_logical(words[2 * a + i2], jnp.int32(a + r)) & 1) == 1, 0.0, NEG)
+                    for i2 in range(2)
+                ]
+                bias_near[i, a, r : r + 1, :] = jnp.where(lane < TILE, fill[0], fill[1]).astype(F32)
+
     for h in range(HEADS_HERE):
         k_t[1, h] = k_all[1, h].T
         v_t[1, h] = v_all[1, h].T
@@ -177,7 +203,7 @@
         cols = head(h)
         here = slice(a * HALF, (a + 1) * HALF)
         keys = slice(a * TILE, a * TILE + SPAN)
-        q = q_v[here, cols]
+        q = q_all[1, h, here, :]
         top = None
         for n in range(3):
             s = lax.dot_general(k_all[n, h, keys, :], q, NT, preferred_element_type=F32)
@@ -194,6 +220,7 @@
             low = e.astype(BF16)
             prob[h, n, a] = low
             out += dot(v_t[n, h, :, keys], low)
+        top_all[1, h : h + 1, here] = top
         inverse = 1.0 / total
         inv_sum[h, :, here] = inverse
         att_t[cols, here] = (out * inverse).astype(BF16)
@@ -205,10 +232,10 @@
             copy.start()
 
     passed((p0[2], p0[3], m0[0], m0[1]), (*p1.values(), *m1.values()))
-    passed((x0[0], x0[1], x0[2]), (p2[2], m2[0], m2[1], p2[1]))
-    passed((x0[3],), (p2[3], m2[2]))
+    passed((x0[0], x0[1], x0[2]), (p2[2], m2[0], m2[1]))
+    passed((x0[3],), (p2[3], m2[2], p2[1]))
+    passed((m0[2], m0[3], p0[0], p0[1]), (x1[3], x2[0]))
     send_halo(True)
-    passed((m0[2], m0[3], p0[0], p0[1]), (x1[3], x2[0]))
 
     for h in range(HEADS_HERE):
         for copy in halo[h]:
@@ -217,12 +244,28 @@
             v_t[n, h] = v_all[n, h].T
         forward(h, 0)
         forward(h, 1)
-    passed((p2[2], m2[0]), (p3[2], m3[0]))
-    passed((p2[3], m2[1]), (p3[3], m3[1]))
+        if h < 2:
+            passed((p2[2 + h], m2[h]), (p3[2 + h], m3[h]))
+    tops = [
+        remote(top_all.at[1], top_all.at[2 * j], stat_s.at[j], stat_r.at[j], ways[j]) for j in range(2)
+    ]
+    for copy in tops:
+        copy.start()
     att[...] = att_t[...].T
     for h in range(HEADS_HERE):
         for n in (0, 2):
             k_t[n, h] = k_all[n, h].T
+
+    def recall(i, h):
+        for a in range(2):
+            here = slice(a * HALF, (a + 1) * HALF)
+            keys = slice(a * TILE, a * TILE + SPAN)
+            s = lax.dot_general(
+                k_all[1, h, keys, :], q_all[2 * i, h, here, :], NT, preferred_element_type=F32
+            ).reshape(3, TILE, HALF)
+            less = bias_near[i, a, 0:3] - top_all[2 * i, h : h + 1, here]
+            e = jnp.exp2(s * (INV_ROOT * LOG2E) + less[:, None, :])
+            prob_near[i, h, a] = e.reshape(SPAN, HALF).astype(BF16)
 
     core_copies = []
 
@@ -244,134 +287,146 @@
         copy.start()
         core_copies.append(copy)
 
+    def share(block):
+        return wg_own[block] + core_in[block].astype(F32)
+
+    chains = {}
+
+    def chain(wave, way, s):
+        step = lax.rem(z + (4 - s if way == 0 else 4 + s), 8)
+        odd = lax.rem(lax.div(step, 4) + y, 2)
+        plane = (1 - odd) * lax.div(y, 2) + odd * lax.div(y_p, 2)
+        if wave == 1:
+            plane = 1 - plane
+        value = share(plane * 8 + step)
+        for before in ((), (), (0, 1) if way == wave else (1,), (2,))[s]:
+            chains[wave, way, before].wait_recv()
+            value += ring_in[wave, way, before].astype(F32)
+        ring_out[wave, way, s] = value.astype(BF16)
+        number = wave * 8 + way * 4 + s
+        if s < 3:
+            copy = remote(
+                ring_out.at[wave, way, s], ring_in.at[wave, way, s], ring_s.at[number], ring_r.at[number],
+                ((z_up2, z_down2) if s == 0 else (z_up, z_down))[way],
+            )
+        else:
+            copy = remote(
+                ring_out.at[wave, way, s], last_in.at[way, x_hi], ring_s.at[number], last_r.at[way * 2 + x_hi],
+                {"lon": plane * 16 + lax.rem(z + (7 if way else 1), 8) * 2 + core},
+            )
+        copy.start()
+        chains[wave, way, s] = copy
+
+    def ring(wave, point):
+        if point == 0:
+            for copy in core_copies[4 * wave : 4 * wave + 4]:
+                copy.wait_recv()
+            chain(wave, wave, 0)
+        for way in range(2):
+            chain(wave, way, point + 1)
+
     local_w.wait()
     use_piece(0, tp)
     use_piece(1, s_x)
     use_piece(2, s_p)
-    use_piece(3, s_m)
+    passed((x1[3], m2[2]), ())
+    use_piece(3, s_px)
+    use_piece(4, s_m)
+    ring(0, 0)
     passed((*p1.values(), *m1.values()), ())
-    use_piece(4, s_2)
-    passed((x1[3], m2[2]), ())
-    use_piece(5, s_px)
+    use_piece(5, s_2)
     passed((x2[0], p2[1]), ())
     use_piece(6, s_mx)
     passed((*p3.values(), *m3.values()), ())
     use_piece(7, s_2x)
 
+    ring(1, 0)
+    x_out[...] = share((1 - x_hi) * 8 + z).astype(BF16)
+    swap = remote(x_out, x_in, x_s.at[0], x_r.at[0], x_far)
+    swap.start()
+
+    tell = []
     for h in range(HEADS_HERE):
         rows = head(h)
         scaled = (do_acc[rows] * inv_sum[h]).astype(BF16)
-        do_t[rows] = scaled
-        delta[h] = jnp.sum(scaled.astype(F32) * att_t[rows].astype(F32), axis=0, keepdims=True)
-    do_n[...] = do_t[...].T
-
-    for copy in core_copies:
+        do_all[1, h] = scaled
+        delta[1, h : h + 1, :] = jnp.sum(scaled.astype(F32) * att_t[rows].astype(F32), axis=0, keepdims=True)
+        for j in range(2):
+            copy = remote(do_all.at[1, h], do_all.at[2 * j, h], tell_s.at[2 * h + j], tell_r.at[2 * h + j], ways[j])
+            copy.start()
+            tell.append(copy)
+    deltas = [
+        remote(delta.at[1], delta.at[2 * j], stat_s.at[2 + j], stat_r.at[2 + j], ways[j]) for j in range(2)
+    ]
+    for copy in deltas:
+        copy.start()
+
+    def spread(e, h, n, a, low, keep):
+        here = slice(a * HALF, (a + 1) * HALF)
+        keys = slice(a * TILE, a * TILE + SPAN)
+        value = v_all[e, h, keys, :]
+        grad = do_all[n, h, :, here]
+        ds = (low.astype(F32) * (dot(value, grad) - delta[n, h : h + 1, here])).astype(BF16)
+        if e == 1:
+            dkey = dot(ds, q_all[n, h, here, :])
+            dval = lax.dot_general(low, grad, NT, preferred_element_type=F32)
+            if keep:
+                pair[h, keys, 0:HEAD_DIM] += dkey
+                pair[h, keys, HEAD_DIM:] += dval
+            elif a == 0:
+                pair[h, keys, 0:HEAD_DIM] = dkey
+                pair[h, keys, HEAD_DIM:] = dval
+            else:
+                pair[h, TILE:SPAN, 0:HEAD_DIM] += dkey[:HALF]
+                pair[h, TILE:SPAN, HEAD_DIM:] += dval[:HALF]
+                pair[h, SPAN:, 0:HEAD_DIM] = dkey[HALF:]
+                pair[h, SPAN:, HEAD_DIM:] = dval[HALF:]
+        return ds
+
+    def own_queries(h):
+        for a in range(2):
+            keys = slice(a * TILE, a * TILE + SPAN)
+            total = None
+            for n in range(3):
+                ds = spread(n, h, 1, a, prob[h, n, a], False)
+                part = dot(k_t[n, h, :, keys], ds)
+                total = part if total is None else total + part
+            dq_ref[a * HALF : (a + 1) * HALF, head(h)] = (total * INV_ROOT).astype(BF16).T
+
+    def near_queries(h):
+        for i in range(2):
+            tell[2 * h + i].wait_recv()
+            for a in range(2):
+                spread(1, h, 2 * i, a, prob_near[i, h, a], True)
+        dk_ref[:, head(h)] = (pair[h, :, 0:HEAD_DIM] * INV_ROOT).astype(BF16)
+        dv_ref[:, head(h)] = pair[h, :, HEAD_DIM:].astype(BF16)
+
+    ring(0, 1)
+    for copy in tops:
         copy.wait_recv()
-
-    def share(block):
-        return wg_own[block] + core_in[block].astype(F32)
-
-    chains = {}
-
-    def chain(way, x, s):
-        first = s == (0 if way == x else 1)
-        step = lax.rem(z + (4 - s if way == 0 else 4 + s), 8)
-        value = share(x * 8 + step)
-        if not first:
-            chains[way, x, s - 1].wait_recv()
-            value += ring_in[way, x, s - 1].astype(F32)
-        ring_out[way, x, s] = value.astype(BF16)
-        number = way * 8 + x * 4 + s
-        if s < 3:
-            copy = remote(
-                ring_out.at[way, x, s], ring_in.at[way, x, s], ring_s.at[number], ring_r.at[number],
-                z_down if way else z_up,
-            )
-        else:
-            copy = remote(
-                ring_out.at[way, x, s], ring_in.at[way, x_hi, s], ring_s.at[number], ring_r.at[way * 8 + x_hi * 4 + s],
-                {"lon": x * 16 + lax.rem(z + (7 if way else 1), 8) * 2 + core},
-            )
-        copy.start()
-        chains[way, x, s] = copy
-
-    def ring(point):
-        chain(0, 0, point)
-        chain(1, 1, point)
-        if point < 3:
-            chain(0, 1, point + 1)
-            chain(1, 0, point + 1)
-
-    pair_copies = {}
-
-    def backward(h, n):
-        cols = head(h)
-        for a in range(2):
-            here = slice(a * HALF, (a + 1) * HALF)
-            keys = slice(a * TILE, a * TILE + SPAN)
-            low = prob[h, n, a]
-            dp = dot(v_all[n, h, keys, :], do_t[cols, here])
-            ds = (low.astype(F32) * (dp - delta[h, :, here])).astype(BF16)
-            dkey = dot(ds, q_v[here, cols])
-            dval = dot(low, do_n[here, cols])
-            dquery = dot(k_t[n, h, :, keys], ds)
-            if n == 0:
-                dq_acc[h, :, here] = dquery
-            else:
-                dq_acc[h, :, here] += dquery
-            if a == 0:
-                pair_acc[0:SPAN, 0:HEAD_DIM] = dkey
-                pair_acc[0:SPAN, HEAD_DIM:] = dval
-            else:
-                pair_acc[TILE:SPAN, 0:HEAD_DIM] += dkey[:HALF]
-                pair_acc[TILE:SPAN, HEAD_DIM:] += dval[:HALF]
-                pair_acc[SPAN:, 0:HEAD_DIM] = dkey[HALF:]
-                pair_acc[SPAN:, HEAD_DIM:] = dval[HALF:]
-        if n == 1:
-            own_pair[h] = pair_acc[...]
-        else:
-            way = n // 2
-            pair_out[way, h] = pair_acc[...].astype(BF16)
-            number = h * 2 + way
-            copy = remote(
-                pair_out.at[way, h], pair_in.at[way, h], pair_s.at[number], pair_r.at[number],
-                right if way else left,
-            )
-            copy.start()
-            pair_copies[h, way] = copy
-
-    ring(0)
-    x_out[...] = share((1 - x_hi) * 8 + z).astype(BF16)
-    swap = remote(x_out, x_in, x_s.at[0], x_r.at[0], x_far)
-    swap.start()
-    backward(0, 0)
-    backward(0, 2)
-    ring(1)
-    backward(1, 0)
-    backward(1, 2)
-    ring(2)
-    backward(2, 0)
-    backward(2, 2)
-    ring(3)
     for h in range(HEADS_HERE):
-        backward(h, 1)
-        dq_ref[:, head(h)] = (dq_acc[h] * INV_ROOT).astype(BF16).T
-
-    for h in range(HEADS_HERE):
-        cols = head(h)
-        for way in range(2):
-            pair_copies[h, way].wait_recv()
-        total = own_pair[h] + pair_in[0, h].astype(F32) + pair_in[1, h].astype(F32)
-        dk_ref[:, cols] = (total[:, :HEAD_DIM] * INV_ROOT).astype(BF16)
-        dv_ref[:, cols] = total[:, HEAD_DIM:].astype(BF16)
+        for i in range(2):
+            ask[h][i].wait_recv()
+            recall(i, h)
+    own_queries(0)
+    ring(1, 1)
+    ring(0, 2)
+    own_queries(1)
+    own_queries(2)
+    ring(1, 2)
+    for copy in deltas:
+        copy.wait_recv()
+    near_queries(0)
+    near_queries(1)
+    near_queries(2)
 
     swap.wait_recv()
     total = share(x_hi * 8 + z) + x_in[...].astype(F32)
     for way in range(2):
         for x in range(2):
-            number = way * 8 + x * 4 + 3
-            pltpu.make_async_copy(ring_out.at[way, x, 3], ring_in.at[way, x, 3], ring_r.at[number]).wait()
-            total += ring_in[way, x, 3].astype(F32)
+            block = last_in.at[way, x]
+            pltpu.make_async_copy(x_out, block, last_r.at[way * 2 + x]).wait()
+            total += last_in[way, x].astype(F32)
     wg_ref[...] = total.astype(BF16)
 
     for copy in sent:
@@ -399,7 +454,7 @@
     dma = pltpu.SemaphoreType.DMA
     block = jax.ShapeDtypeStruct((TOK, COLS), BF16)
     scratch = [
-        V((TOK, COLS), BF16),
+        V((3, HEADS_HERE, TOK, HEAD_DIM), BF16),
         V((3, HEADS_HERE, TOK, HEAD_DIM), BF16),
         V((3, HEADS_HERE, TOK, HEAD_DIM), BF16),
         V((TOK, COLS), BF16),
@@ -408,34 +463,36 @@
         V((3, HEADS_HERE, HEAD_DIM, TOK), BF16),
         V((3, HEADS_HERE, HEAD_DIM, TOK), BF16),
         V((HEADS_HERE, 3, 2, SPAN, HALF), BF16),
+        V((2, HEADS_HERE, 2, SPAN, HALF), BF16),
         V((3, SPAN, HALF), F32),
         V((2, 16, HALF), F32),
+        V((2, 2, 8, HALF), F32),
+        V((3, 8, TOK), F32),
         V((COLS, TOK), BF16),
         V((TOK, COLS), BF16),
         V((HEADS_HERE, 1, TOK), F32),
-        V((HEADS_HERE, 1, TOK), F32),
+        V((3, 8, TOK), F32),
         V((COLS, TOK), F32),
-        V((COLS, TOK), BF16),
-        V((TOK, COLS), BF16),
-        V((HEADS_HERE, HEAD_DIM, TOK), F32),
-        V((TOK, HALF), F32),
+        V((3, HEADS_HERE, HEAD_DIM, TOK), BF16),
         V((HEADS_HERE, TOK, HALF), F32),
-        V((2, HEADS_HERE, TOK, HALF), BF16),
-        V((2, HEADS_HERE, TOK, HALF), BF16),
         V((COLS, COLS), F32),
         V((16, STRIP, COLS), F32),
         V((16, STRIP, COLS), BF16),
         V((16, STRIP, COLS), BF16),
         V((2, 2, 4, STRIP, COLS), BF16),
         V((2, 2, 4, STRIP, COLS), BF16),
+        V((2, 2, STRIP, COLS), BF16),
         V((STRIP, COLS), BF16),
         V((STRIP, COLS), BF16),
-        dma((9,)),
+        dma((11,)),
         dma((12,)), dma((12,)),
         dma((GATHERS,)), dma((GATHERS,)),
         dma((6,)), dma((6,)),
+        dma((4,)), dma((4,)),
+        dma((6,)), dma((6,)),
         dma((8,)), dma((8,)),
         dma((16,)), dma((16,)),
+        dma((4,)),
         dma((1,)), dma((1,)),
     ]
     dq, dk, dv, wg = pl.pallas_call(

time: 69.3 us -> 67.5 us (0.974)
  the two profiles are of different devices: /device:TPU:1 before, /device:TPU:6 now
where the time goes in v3:
time: 67.5 us; the launch traced here: 67.4 us
  Pallas kernels  66.6 us (99%)
  between operations  0.8 us (1%)
    pallas_call x1, Pallas kernels, body(): pl.pallas_call(kernel, out_shape=(block, block, block, jax.ShapeDtypeStru...  64.5 us
    pallas_call x1, Pallas kernels, body(): pl.pallas_call(copy_out, out_shape=tuple((jax.ShapeDtypeStruct(r.shape, B...  2.09 us

profile of v3, /device:TPU:6, one launch (start us, length us, event | category | flops | bytes accessed | tf_op | source)
XLA Modules:
  0.0 67.4 jit_solution(5195033713585006899)
XLA Ops:
  0.6 64.5 %shard_map.102 = (bf16[512,384]{1,0:T(8,128)(2,1)}, bf16[512,384]{1,0:T(8,128)(2,1)}, bf16[512,384]{1,0:T(8,128)(2,1)}, bf16[96,384]{1,0:T(8,128)(2,1)}) custom-call(s32[9,128]{1,0:T(8,128)} %bitcast.2, s32[128]{0:T(128)} %cnt_ref.1, bf16[512,384]{1,0:T(8,128)(2,1)} %q_hbm.1, bf16[512,384]{1,0:T(8,128)(2,1)} %k_hbm.1, bf16[512,384]{1,0:T(8,128)(2,1)} %v_hbm.1, ...), custom_call_target="tpu_custom_call" | custom-call | tf_op jit(solution)/shard_map/pallas_call | solution.py:498
  65.1 2.1 %shard_map.103 = (bf16[512,384]{1,0:T(8,128)(2,1)}, bf16[512,384]{1,0:T(8,128)(2,1)}, bf16[512,384]{1,0:T(8,128)(2,1)}, bf16[96,384]{1,0:T(8,128)(2,1)}) custom-call(bf16[512,384]{1,0:T(8,128)(2,1)} %get-tuple-element.12.refs_0_, bf16[512,384]{1,0:T(8,128)(2,1)} %get-tuple-element.13.refs_1_, bf16[512,384]{1,0:T(8,128)(2,1)} %get-tuple-element.14.refs_2_, ...), custom_call_target="tpu_custom_call" | custom-call | tf_op jit(solution)/shard_map/pallas_call | solution.py:509

commit v4 on v3

--- a/solution.py
+++ b/solution.py
@@ -412,8 +412,8 @@
     ring(1, 1)
     ring(0, 2)
     own_queries(1)
+    ring(1, 2)
     own_queries(2)
-    ring(1, 2)
     for copy in deltas:
         copy.wait_recv()
     near_queries(0)

time: 67.5 us -> 66.5 us (0.985)
  the two profiles are of different devices: /device:TPU:6 before, /device:TPU:1 now
where the time goes in v4:
time: 66.5 us; the launch traced here: 66.2 us
  Pallas kernels  65.4 us (98%)
  between operations  0.8 us (1%)
    pallas_call x1, Pallas kernels, body(): pl.pallas_call(kernel, out_shape=(block, block, block, jax.ShapeDtypeStru...  63.4 us
    pallas_call x1, Pallas kernels, body(): pl.pallas_call(copy_out, out_shape=tuple((jax.ShapeDtypeStruct(r.shape, B...  2.09 us

profile of v4, /device:TPU:1, one launch (start us, length us, event | category | flops | bytes accessed | tf_op | source)
XLA Modules:
  0.0 66.2 jit_solution(9540531486661566045)
XLA Ops:
  0.6 63.4 %shard_map.102 = (bf16[512,384]{1,0:T(8,128)(2,1)}, bf16[512,384]{1,0:T(8,128)(2,1)}, bf16[512,384]{1,0:T(8,128)(2,1)}, bf16[96,384]{1,0:T(8,128)(2,1)}) custom-call(s32[9,128]{1,0:T(8,128)} %bitcast.2, s32[128]{0:T(128)} %cnt_ref.1, bf16[512,384]{1,0:T(8,128)(2,1)} %q_hbm.1, bf16[512,384]{1,0:T(8,128)(2,1)} %k_hbm.1, bf16[512,384]{1,0:T(8,128)(2,1)} %v_hbm.1, ...), custom_call_target="tpu_custom_call" | custom-call | tf_op jit(solution)/shard_map/pallas_call | solution.py:498
  64.0 2.1 %shard_map.103 = (bf16[512,384]{1,0:T(8,128)(2,1)}, bf16[512,384]{1,0:T(8,128)(2,1)}, bf16[512,384]{1,0:T(8,128)(2,1)}, bf16[96,384]{1,0:T(8,128)(2,1)}) custom-call(bf16[512,384]{1,0:T(8,128)(2,1)} %get-tuple-element.12.refs_0_, bf16[512,384]{1,0:T(8,128)(2,1)} %get-tuple-element.13.refs_1_, bf16[512,384]{1,0:T(8,128)(2,1)} %get-tuple-element.14.refs_2_, ...), custom_call_target="tpu_custom_call" | custom-call | tf_op jit(solution)/shard_map/pallas_call | solution.py:509
